TPU v7x, 32 devices: a whole 2x2x4 slice. The times are simulated.
32 devices in a mesh: outer: 8 (over z, x), inner: 4 (over y, core).
Axes of the slice: x: 2, y: 2, z: 4, core: 2. Of those that a mesh axis runs over, the one named last changes fastest.
Arguments:
- query: bfloat16 [4096, 32, 128], P(('outer', 'inner')), may hold values from -6 to 6
- keys: bfloat16 [4096, 32, 128], P(('outer', 'inner')), may hold values from -6 to 6
- value: bfloat16 [4096, 32, 128], P(('outer', 'inner')), may hold values from -6 to 6
- beta: bfloat16 [4096, 32], P(('outer', 'inner')), may hold values from 0 to 1, as said below
Outputs:
- mixed: bfloat16 [4096, 32, 128], P(('outer', 'inner'))
Inputs may be any that keep to these rules, and one draw needn't show every extreme that they name: `beta`: each gate lies strictly between 0 and 1.
All inputs are finite; a program needn't handle non-finite values.
Results may differ from a plain program's by a relative error of at most 0.001.
Values may be sent and summed in bfloat16 or wider, within the bound.
A program may use at most 128 MiB of HBM per device.

v0:
```python
import functools

import jax
import jax.numpy as jnp
from jax import lax
from jax.experimental import pallas as pl
from jax.experimental.pallas import tpu as pltpu
from jax.sharding import PartitionSpec as P

SPAN = 128
GROUP = 4
F32 = jnp.float32
BF16 = jnp.bfloat16


def halves(x):
    high = x.astype(BF16)
    return high, (x - high.astype(F32)).astype(BF16)


def dot(a, b):
    return jnp.dot(a, b, preferred_element_type=F32)


def dot_halves(a, b):
    (ah, al), (bh, bl) = a, b
    return dot(jnp.concatenate([ah, al], 1), jnp.concatenate([bh, bh], 0)) + dot(ah, bl)


def dot_exact(a, b):
    ah, al = a
    return dot(jnp.concatenate([ah, al], 1), jnp.concatenate([b, b], 0))


def block_map(keys, value, brow, rows, cols):
    eye = rows == cols
    width = keys[0].shape[1]
    count = range(len(keys))
    gram = [lax.dot_general(x, x, (((1,), (1,)), ((), ())), preferred_element_type=F32) for x in keys]
    kf = [x.astype(F32) for x in keys]
    krow = [lax.rsqrt(jnp.sum(jnp.where(eye, x, 0.0), axis=0, keepdims=True) + 1e-6) for x in gram]
    kcol = [lax.rsqrt(jnp.sum(x * x, axis=1, keepdims=True) + 1e-6) for x in kf]
    bcol = [jnp.sum(jnp.where(eye, x, 0.0), axis=1, keepdims=True) for x in brow]
    lower = [jnp.where(rows > cols, gram[i] * (bcol[i] * kcol[i]) * krow[i], 0.0) for i in count]
    split = [halves(x) for x in lower]

    def merge_mask(level):
        return ((rows >> (level + 1)) == (cols >> (level + 1))) & (((rows >> level) & 1) == 1) & (((cols >> level) & 1) == 0)

    first = merge_mask(0)
    inverse = [jnp.where(eye, 1.0, 0.0) - jnp.where(first, x, 0.0) for x in lower]
    zero = jnp.zeros((), BF16)
    for level in range(1, (SPAN - 1).bit_length()):
        mask = merge_mask(level)
        part = [(jnp.where(mask, h, zero), jnp.where(mask, l, zero)) for h, l in split]
        inv = [halves(x) for x in inverse]
        inner = [dot_halves(part[i], inv[i]) for i in count]
        inner = [halves(x) for x in inner]
        change = [dot_halves(inv[i], inner[i]) for i in count]
        inverse = [inverse[i] - change[i] for i in count]
    for_keys = [halves(inverse[i] * (brow[i] * krow[i])) for i in count]
    for_value = [halves(inverse[i] * brow[i]) for i in count]
    weights = [dot_exact(for_keys[i], keys[i]) for i in count]
    updates = [dot_exact(for_value[i], value[i]) for i in count]
    solved = [jnp.concatenate([weights[i], updates[i]], 1) for i in count]
    scaled = [halves(solved[i] * kcol[i]) for i in count]
    written = [
        lax.dot_general(
            jnp.concatenate([keys[i], keys[i]], 0),
            jnp.concatenate(scaled[i], 0),
            (((0,), (0,)), ((), ())),
            preferred_element_type=F32,
        )
        for i in count
    ]
    trans = [jnp.where(eye, 1.0, 0.0) - x[:, :width] for x in written]
    return trans, [x[:, width:] for x in written], solved, krow


def block_reads(query, keys, solved, krow, rows, cols):
    width = keys[0].shape[1]
    count = range(len(keys))
    raw = [
        lax.dot_general(q, k, (((1,), (1,)), ((), ())), preferred_element_type=F32) for q, k in zip(query, keys)
    ]
    qf = [x.astype(F32) for x in query]
    qcol = [lax.rsqrt(jnp.sum(x * x, axis=1, keepdims=True) + 1e-6) for x in qf]
    scores = [halves(jnp.where(rows >= cols, raw[i] * qcol[i] * krow[i], 0.0)) for i in count]
    solved = [halves(x) for x in solved]
    seen = [dot_halves(scores[i], solved[i]) for i in count]
    return [qf[i] * qcol[i] - seen[i][:, :width] for i in count], [x[:, width:] for x in seen]


def kernel(outer, inner, q_ref, k_ref, v_ref, b_ref, o_ref, pair, outgoing, solved, norms, whole, jump, first, came, goes, middle, side, ab_send, ab_recv, chain_send, chain_recv, side_send, side_recv):
    heads = q_ref.shape[0]
    owned = heads // 2
    each = GROUP // 2
    groups = owned // each
    total = outer * inner
    me = lax.axis_index("outer") * inner + lax.axis_index("inner")
    core, chip, chips = lax.rem(me, 2), me // 2, total // 2
    after, before, sibling = lax.rem(me + 2, total), lax.rem(me + total - 2, total), me + 1 - 2 * core

    def place(index):
        return (index // inner, lax.rem(index, inner))

    barrier = pltpu.get_barrier_semaphore()
    for other in (after, before, sibling):
        pl.semaphore_signal(barrier, inc=1, device_id=place(other), device_id_type=pl.DeviceIdType.MESH)
    pl.semaphore_wait(barrier, 3)

    def send(src, dst, send_sem, recv_sem, to):
        return pltpu.make_async_remote_copy(
            src_ref=src,
            dst_ref=dst,
            send_sem=send_sem,
            recv_sem=recv_sem,
            device_id=place(to),
            device_id_type=pl.DeviceIdType.MESH,
        )

    def give(m):
        return send(outgoing.at[m], pair.at[m, core], ab_send.at[m], ab_recv.at[m], sibling)

    def take(m):
        return send(outgoing.at[m], pair.at[m, 1 - core], ab_send.at[m], ab_recv.at[m], sibling)

    def hop(m):
        return send(goes.at[m], came.at[m], chain_send.at[m], chain_recv.at[m], after)

    def aside(src, m):
        return send(src.at[m], side.at[m], side_send.at[m], side_recv.at[m], sibling)

    @pl.when(chip == 0)
    def _():
        came[...] = jnp.zeros_like(came)

    def masks():
        return [lax.broadcasted_iota(jnp.int32, (SPAN, SPAN), axis) for axis in (0, 1)]

    def group(g):
        ms = [g * each + j for j in range(each)]
        return ms, [core * owned + m for m in ms], [(1 - core) * owned + m for m in ms]

    def prepare(g):
        ms, mine, theirs = group(g)
        hs = mine + theirs
        a, b, wu, krow = block_map(*([ref[h] for h in hs] for ref in (k_ref, v_ref, b_ref)), *masks())
        for j, h in enumerate(hs):
            solved[h] = wu[j]
            norms[h] = krow[j]
        for j, m in enumerate(ms):
            outgoing[m, :SPAN] = a[each + j]
            outgoing[m, SPAN:] = b[each + j]
        for m in ms:
            give(m).start()
        for j, m in enumerate(ms):
            pair[m, core, :SPAN] = a[j]
            pair[m, core, SPAN:] = b[j]

    def compose(g):
        ms, _, _ = group(g)
        for m in ms:
            take(m).wait_recv()
        early = [halves(jnp.concatenate([pair[m, 0, :SPAN], pair[m, 0, SPAN:]], 1)) for m in ms]
        late = [halves(pair[m, 1, :SPAN]) for m in ms]
        both = [dot_halves(x, y) for x, y in zip(late, early)]
        for j, m in enumerate(ms):
            whole[m] = jnp.concatenate(halves(both[j][:, :SPAN]), 1)
            jump[m] = both[j][:, SPAN:] + pair[m, 1, SPAN:]
            first[m] = jnp.concatenate([x[:, :SPAN] for x in early[j]], 1)

    def apply(linear, state, constant):
        high, low = state
        return constant + dot(linear, jnp.concatenate([high, high], 0)) + dot(linear[:, :SPAN], low)

    def pass_on(g):
        ms, _, _ = group(g)
        for m in ms:
            @pl.when(chip > 0)
            def _():
                hop(m).wait_recv()

            goes[m] = apply(whole[m], halves(came[m]), jump[m])

            @pl.when(chip < chips - 1)
            def _():
                hop(m).start()

            @pl.when(core == 1)
            def _():
                aside(came, m).start()

        for m in ms:
            middle[m] = apply(first[m], halves(came[m]), pair[m, 0, SPAN:])

        @pl.when(core == 0)
        def _():
            for m in ms:
                aside(middle, m).start()

    def read_terms(g):
        _, mine, theirs = group(g)
        hs = mine + theirs
        p, o = block_reads([q_ref[h] for h in hs], [k_ref[h] for h in hs], [solved[h] for h in hs], [norms[h] for h in hs], *masks())
        for j, h in enumerate(hs):
            solved[h] = jnp.concatenate([p[j], o[j]], 1)

    def put(hs, states):
        terms = [solved[h] for h in hs]
        states = [halves(x) for x in states]
        mixed = [x[:, SPAN:] + dot_halves(halves(x[:, :SPAN]), y) for x, y in zip(terms, states)]
        for h, x in zip(hs, mixed):
            o_ref[h] = x.astype(BF16)

    def finish(g):
        ms, mine, theirs = group(g)
        put(mine, [jnp.where(core == 0, came[m], middle[m]) for m in ms])
        for m in ms:
            aside(middle, m).wait_recv()
        put(theirs, [side[m] for m in ms])

    ahead = jnp.minimum(groups, 1 + chip // 2)
    late = jnp.where(chip < chips // 2, groups + ahead, 0)
    last = jnp.maximum(late, ahead + 1)

    def step(i, carry):
        @pl.when(i < groups)
        def _():
            prepare(i)

        @pl.when((i >= late) & (i < late + groups))
        def _():
            read_terms(i - late)

        @pl.when((i >= 1) & (i <= groups))
        def _():
            compose(i - 1)

        @pl.when((i >= ahead) & (i < ahead + groups))
        def _():
            pass_on(i - ahead)

        @pl.when((i >= last) & (i < last + groups))
        def _():
            finish(i - last)

        return carry

    lax.fori_loop(0, groups + last, step, 0)

    def drain(m, carry):
        give(m).wait_send()
        aside(middle, m).wait_send()

        @pl.when(chip < chips - 1)
        def _():
            hop(m).wait_send()

        return carry

    lax.fori_loop(0, owned, drain, 0)


def shards(outer, inner, query, keys, value, beta):
    tokens, heads, width = query.shape
    major = [jnp.transpose(x, (1, 0, 2)) for x in (query, keys, value)]
    gates = jnp.transpose(beta.astype(F32), (1, 0)).reshape(heads, 1, tokens)
    half = heads // 2
    vmem = pl.BlockSpec(memory_space=pltpu.VMEM)
    mixed = pl.pallas_call(
        functools.partial(kernel, outer, inner),
        out_shape=jax.ShapeDtypeStruct((heads, tokens, width), BF16),
        in_specs=[vmem] * 4,
        out_specs=vmem,
        scratch_shapes=[
            pltpu.VMEM((half, 2, 2 * width, width), F32),
            pltpu.VMEM((half, 2 * width, width), F32),
            pltpu.VMEM((heads, tokens, 2 * width), F32),
            pltpu.VMEM((heads, 1, tokens), F32),
            pltpu.VMEM((half, width, 2 * width), BF16),
            pltpu.VMEM((half, width, width), F32),
            pltpu.VMEM((half, width, 2 * width), BF16),
            *[pltpu.VMEM((half, width, width), F32)] * 4,
            *[pltpu.SemaphoreType.DMA((half,))] * 6,
        ],
        compiler_params=pltpu.CompilerParams(
            collective_id=0, has_side_effects=True, vmem_limit_bytes=40 * 2**20
        ),
        cost_estimate=pl.CostEstimate(flops=heads * 60 * 2 * 128**3, bytes_accessed=2**22, transcendentals=0),
    )(*major, gates)
    return jnp.transpose(mixed, (1, 0, 2))


def solution(mesh):
    placed = P(("outer", "inner"), None, None)
    return jax.shard_map(
        functools.partial(shards, mesh.shape["outer"], mesh.shape["inner"]),
        mesh=mesh,
        in_specs=(placed, placed, placed, P(("outer", "inner"), None)),
        out_specs=placed,
        check_vma=False,
    )
```

profile of v0, /device:TPU:31, one launch (start us, length us, event | category | flops | bytes accessed | tf_op | source)
XLA Modules:
  0.0 104.6 jit_solution(15003889663388299467)
XLA Ops:
  0.0 0.7 reshape.9
  0.7 0.0 copy-start
  0.7 0.0 copy-start.1
  0.7 1.8 %copy.12 = bf16[128,32,128]{2,0,1:T(8,128)(2,1)S(1)} copy(bf16[128,32,128]{2,1,0:T(8,128)(2,1)} %param.4) | data formatting | bytes 2097152 | tf_op args[0]
  2.5 0.0 copy-done
  2.5 0.1 copy-done.1
  2.6 0.8 copy_bitcast_fusion
  3.4 99.6 %shard_map.46 = bf16[32,128,128]{2,1,0:T(8,128)(2,1)S(1)} custom-call(bf16[32,128,128]{2,1,0:T(8,128)(2,1)S(1)} %bitcast.11, bf16[32,128,128]{2,1,0:T(8,128)(2,1)S(1)} %get-tuple-element.6.k_ref, bf16[32,128,128]{2,1,0:T(8,128)(2,1)S(1)} %get-tuple-element.5.v_ref, f32[32,1,128]{2,1,0:T(1,128)S(1)} %bitcast.13), custom_call_target="tpu_custom_call" | custom-call | flops 8053063680 | bytes 4194304 | tf_op jit(solution)/shard_map/pallas_call | solution.py:271
  103.0 1.6 %copy.8 = bf16[128,32,128]{2,1,0:T(8,128)(2,1)} copy(bf16[128,32,128]{2,0,1:T(8,128)(2,1)S(1)} %bitcast.12) | data formatting | bytes 2097152 | tf_op jit(solution)/shard_map/transpose | solution.py:292
Async XLA Ops:
  0.7 1.8 %copy-start = (bf16[128,32,128]{2,1,0:T(8,128)(2,1)S(1)}, bf16[128,32,128]{2,1,0:T(8,128)(2,1)}, u32[]{:S(2)}) copy-start(bf16[128,32,128]{2,1,0:T(8,128)(2,1)} %param.6) | copy-start | bytes 3145732
  0.7 1.9 %copy-start.1 = (bf16[128,32,128]{2,1,0:T(8,128)(2,1)S(1)}, bf16[128,32,128]{2,1,0:T(8,128)(2,1)}, u32[]{:S(2)}) copy-start(bf16[128,32,128]{2,1,0:T(8,128)(2,1)} %param.5) | copy-start | bytes 3145732
where the time goes:
time: 105 us
  Pallas kernels  99.6 us (95%)
  local copies, waits for them, and re-layouts  4.31 us (4%)
    pallas_call x1, Pallas kernels, shards(): pl.pallas_call(functools.partial(kernel, outer, inner), out_shape=jax.Sha...  99.6 us

commit v1 on v0

--- a/solution.py
+++ b/solution.py
@@ -8,7 +8,6 @@
 from jax.sharding import PartitionSpec as P
 
 SPAN = 128
-GROUP = 4
 F32 = jnp.float32
 BF16 = jnp.bfloat16
 
@@ -91,23 +90,32 @@
     return [qf[i] * qcol[i] - seen[i][:, :width] for i in count], [x[:, width:] for x in seen]
 
 
-def kernel(outer, inner, q_ref, k_ref, v_ref, b_ref, o_ref, pair, outgoing, solved, norms, whole, jump, first, came, goes, middle, side, ab_send, ab_recv, chain_send, chain_recv, side_send, side_recv):
+def kernel(
+    outer, inner, q_ref, k_ref, v_ref, b_ref, o_ref,
+    pair, outgoing, solved, norms, first, chip_map, cross, whole, jump, inside, came, goes, start, chip_start, middle, side,
+    ab_send, ab_recv, side_send, side_recv, cross_send, cross_recv, down_send, down_recv, chain_send, chain_recv,
+):
     heads = q_ref.shape[0]
     owned = heads // 2
-    each = GROUP // 2
-    groups = owned // each
+    chips = inner // 2
+    groups = owned // chips
     total = outer * inner
-    me = lax.axis_index("outer") * inner + lax.axis_index("inner")
-    core, chip, chips = lax.rem(me, 2), me // 2, total // 2
-    after, before, sibling = lax.rem(me + 2, total), lax.rem(me + total - 2, total), me + 1 - 2 * core
-
-    def place(index):
-        return (index // inner, lax.rem(index, inner))
+    stage, place_in = lax.axis_index("outer"), lax.axis_index("inner")
+    core, chip = lax.rem(place_in, 2), place_in // 2
+    after, before = lax.rem(stage + 1, outer), lax.rem(stage + outer - 1, outer)
+    sibling = (stage, place_in + 1 - 2 * core)
+
+    def turned(d):
+        return lax.rem(chip + d, chips)
+
+    def beside(other):
+        return (stage, other * 2 + core)
 
     barrier = pltpu.get_barrier_semaphore()
-    for other in (after, before, sibling):
-        pl.semaphore_signal(barrier, inc=1, device_id=place(other), device_id_type=pl.DeviceIdType.MESH)
-    pl.semaphore_wait(barrier, 3)
+    met = [(after, place_in), (before, place_in), sibling] + [beside(turned(d)) for d in range(1, chips)]
+    for other in met:
+        pl.semaphore_signal(barrier, inc=1, device_id=other, device_id_type=pl.DeviceIdType.MESH)
+    pl.semaphore_wait(barrier, len(met))
 
     def send(src, dst, send_sem, recv_sem, to):
         return pltpu.make_async_remote_copy(
@@ -115,23 +123,36 @@
             dst_ref=dst,
             send_sem=send_sem,
             recv_sem=recv_sem,
-            device_id=place(to),
+            device_id=to,
             device_id_type=pl.DeviceIdType.MESH,
         )
 
     def give(m):
         return send(outgoing.at[m], pair.at[m, core], ab_send.at[m], ab_recv.at[m], sibling)
 
-    def take(m):
-        return send(outgoing.at[m], pair.at[m, 1 - core], ab_send.at[m], ab_recv.at[m], sibling)
-
-    def hop(m):
-        return send(goes.at[m], came.at[m], chain_send.at[m], chain_recv.at[m], after)
+    def across(g, d):
+        other, at = turned(d), g * (chips - 1) + d - 1
+        return send(chip_map.at[other * groups + g], cross.at[g, chip], cross_send.at[at], cross_recv.at[at], beside(other))
+
+    def across_in(g, d):
+        other, at = turned(chips - d), g * (chips - 1) + d - 1
+        return send(chip_map.at[g], cross.at[g, other], cross_send.at[at], cross_recv.at[at], beside(other))
+
+    def hop(g):
+        return send(goes.at[g], came.at[g], chain_send.at[g], chain_recv.at[g], (after, place_in))
+
+    def down(g, d):
+        other, at = turned(d), g * (chips - 1) + d - 1
+        return send(start.at[g, other], chip_start.at[chip * groups + g], down_send.at[at], down_recv.at[at], beside(other))
+
+    def down_in(g, d):
+        other, at = turned(chips - d), g * (chips - 1) + d - 1
+        return send(start.at[g, other], chip_start.at[other * groups + g], down_send.at[at], down_recv.at[at], beside(other))
 
     def aside(src, m):
         return send(src.at[m], side.at[m], side_send.at[m], side_recv.at[m], sibling)
 
-    @pl.when(chip == 0)
+    @pl.when(stage == 0)
     def _():
         came[...] = jnp.zeros_like(came)
 
@@ -139,7 +160,7 @@
         return [lax.broadcasted_iota(jnp.int32, (SPAN, SPAN), axis) for axis in (0, 1)]
 
     def group(g):
-        ms = [g * each + j for j in range(each)]
+        ms = [c * groups + g for c in range(chips)]
         return ms, [core * owned + m for m in ms], [(1 - core) * owned + m for m in ms]
 
     def prepare(g):
@@ -150,8 +171,8 @@
             solved[h] = wu[j]
             norms[h] = krow[j]
         for j, m in enumerate(ms):
-            outgoing[m, :SPAN] = a[each + j]
-            outgoing[m, SPAN:] = b[each + j]
+            outgoing[m, :SPAN] = a[chips + j]
+            outgoing[m, SPAN:] = b[chips + j]
         for m in ms:
             give(m).start()
         for j, m in enumerate(ms):
@@ -161,38 +182,71 @@
     def compose(g):
         ms, _, _ = group(g)
         for m in ms:
-            take(m).wait_recv()
+            send(outgoing.at[m], pair.at[m, 1 - core], ab_send.at[m], ab_recv.at[m], sibling).wait_recv()
         early = [halves(jnp.concatenate([pair[m, 0, :SPAN], pair[m, 0, SPAN:]], 1)) for m in ms]
         late = [halves(pair[m, 1, :SPAN]) for m in ms]
         both = [dot_halves(x, y) for x, y in zip(late, early)]
         for j, m in enumerate(ms):
-            whole[m] = jnp.concatenate(halves(both[j][:, :SPAN]), 1)
-            jump[m] = both[j][:, SPAN:] + pair[m, 1, SPAN:]
+            chip_map[m, :SPAN] = both[j][:, :SPAN]
+            chip_map[m, SPAN:] = both[j][:, SPAN:] + pair[m, 1, SPAN:]
+        for d in range(1, chips):
+            across(g, d).start()
+        for j, m in enumerate(ms):
             first[m] = jnp.concatenate([x[:, :SPAN] for x in early[j]], 1)
+        cross[g, chip] = chip_map[chip * groups + g]
+
+    def compose_chips(g):
+        for d in range(1, chips):
+            across_in(g, d).wait_recv()
+        both = jnp.concatenate([cross[g, 0, :SPAN], cross[g, 0, SPAN:]], 1)
+        for c in range(1, chips):
+            split = halves(both)
+            if c == 1:
+                inside[g, 0] = jnp.concatenate([x[:, :SPAN] for x in split], 1)
+            late = halves(cross[g, c, :SPAN])
+            if c < chips - 1:
+                inside[g, c] = jnp.concatenate(late, 1)
+            moved = dot_halves(late, split)
+            both = jnp.concatenate([moved[:, :SPAN], moved[:, SPAN:] + cross[g, c, SPAN:]], 1)
+        whole[g] = jnp.concatenate(halves(both[:, :SPAN]), 1)
+        jump[g] = both[:, SPAN:]
 
     def apply(linear, state, constant):
-        high, low = state
+        high, low = halves(state)
         return constant + dot(linear, jnp.concatenate([high, high], 0)) + dot(linear[:, :SPAN], low)
 
     def pass_on(g):
+        @pl.when(stage > 0)
+        def _():
+            hop(g).wait_recv()
+
+        state = came[g]
+        goes[g] = apply(whole[g], state, jump[g])
+
+        @pl.when(stage < outer - 1)
+        def _():
+            hop(g).start()
+
+        for c in range(chips):
+            start[g, c] = state
+            if c < chips - 1:
+                state = apply(inside[g, c], state, cross[g, c, SPAN:])
+        for d in range(1, chips):
+            down(g, d).start()
+        chip_start[chip * groups + g] = start[g, chip]
+
+    def spread(g):
         ms, _, _ = group(g)
+        for d in range(1, chips):
+            down_in(g, d).wait_recv()
+
+        @pl.when(core == 1)
+        def _():
+            for m in ms:
+                aside(chip_start, m).start()
+
         for m in ms:
-            @pl.when(chip > 0)
-            def _():
-                hop(m).wait_recv()
-
-            goes[m] = apply(whole[m], halves(came[m]), jump[m])
-
-            @pl.when(chip < chips - 1)
-            def _():
-                hop(m).start()
-
-            @pl.when(core == 1)
-            def _():
-                aside(came, m).start()
-
-        for m in ms:
-            middle[m] = apply(first[m], halves(came[m]), pair[m, 0, SPAN:])
+            middle[m] = apply(first[m], chip_start[m], pair[m, 0, SPAN:])
 
         @pl.when(core == 0)
         def _():
@@ -202,7 +256,7 @@
     def read_terms(g):
         _, mine, theirs = group(g)
         hs = mine + theirs
-        p, o = block_reads([q_ref[h] for h in hs], [k_ref[h] for h in hs], [solved[h] for h in hs], [norms[h] for h in hs], *masks())
+        p, o = block_reads(*([ref[h] for h in hs] for ref in (q_ref, k_ref, solved, norms)), *masks())
         for j, h in enumerate(hs):
             solved[h] = jnp.concatenate([p[j], o[j]], 1)
 
@@ -215,36 +269,28 @@
 
     def finish(g):
         ms, mine, theirs = group(g)
-        put(mine, [jnp.where(core == 0, came[m], middle[m]) for m in ms])
+        put(mine, [jnp.where(core == 0, chip_start[m], middle[m]) for m in ms])
         for m in ms:
             aside(middle, m).wait_recv()
         put(theirs, [side[m] for m in ms])
 
-    ahead = jnp.minimum(groups, 1 + chip // 2)
-    late = jnp.where(chip < chips // 2, groups + ahead, 0)
-    last = jnp.maximum(late, ahead + 1)
+    ahead = jnp.minimum(groups, 2 + 3 * stage // 4)
+    late = jnp.where(stage < outer // 4, groups + ahead, 0)
+    last = jnp.maximum(late, ahead + 2)
 
     def step(i, carry):
-        @pl.when(i < groups)
-        def _():
-            prepare(i)
-
-        @pl.when((i >= late) & (i < late + groups))
-        def _():
-            read_terms(i - late)
-
-        @pl.when((i >= 1) & (i <= groups))
-        def _():
-            compose(i - 1)
-
-        @pl.when((i >= ahead) & (i < ahead + groups))
-        def _():
-            pass_on(i - ahead)
-
-        @pl.when((i >= last) & (i < last + groups))
-        def _():
-            finish(i - last)
-
+        def at(delay, do):
+            @pl.when((i >= delay) & (i < delay + groups))
+            def _():
+                do(i - delay)
+
+        at(0, prepare)
+        at(late, read_terms)
+        at(1, compose)
+        at(2, compose_chips)
+        at(ahead, pass_on)
+        at(ahead + 1, spread)
+        at(last, finish)
         return carry
 
     lax.fori_loop(0, groups + last, step, 0)
@@ -252,21 +298,30 @@
     def drain(m, carry):
         give(m).wait_send()
         aside(middle, m).wait_send()
-
-        @pl.when(chip < chips - 1)
-        def _():
-            hop(m).wait_send()
-
         return carry
 
     lax.fori_loop(0, owned, drain, 0)
+
+    def drain_chain(g, carry):
+        for d in range(1, chips):
+            across(g, d).wait_send()
+            down(g, d).wait_send()
+
+        @pl.when(stage < outer - 1)
+        def _():
+            hop(g).wait_send()
+
+        return carry
+
+    lax.fori_loop(0, groups, drain_chain, 0)
 
 
 def shards(outer, inner, query, keys, value, beta):
     tokens, heads, width = query.shape
     major = [jnp.transpose(x, (1, 0, 2)) for x in (query, keys, value)]
     gates = jnp.transpose(beta.astype(F32), (1, 0)).reshape(heads, 1, tokens)
-    half = heads // 2
+    half, chips = heads // 2, inner // 2
+    groups = half // chips
     vmem = pl.BlockSpec(memory_space=pltpu.VMEM)
     mixed = pl.pallas_call(
         functools.partial(kernel, outer, inner),
@@ -279,10 +334,18 @@
             pltpu.VMEM((heads, tokens, 2 * width), F32),
             pltpu.VMEM((heads, 1, tokens), F32),
             pltpu.VMEM((half, width, 2 * width), BF16),
-            pltpu.VMEM((half, width, width), F32),
-            pltpu.VMEM((half, width, 2 * width), BF16),
-            *[pltpu.VMEM((half, width, width), F32)] * 4,
-            *[pltpu.SemaphoreType.DMA((half,))] * 6,
+            pltpu.VMEM((half, 2 * width, width), F32),
+            pltpu.VMEM((groups, chips, 2 * width, width), F32),
+            pltpu.VMEM((groups, width, 2 * width), BF16),
+            pltpu.VMEM((groups, width, width), F32),
+            pltpu.VMEM((groups, chips - 1, width, 2 * width), BF16),
+            pltpu.VMEM((groups, width, width), F32),
+            pltpu.VMEM((groups, width, width), F32),
+            pltpu.VMEM((groups, chips, width, width), F32),
+            *[pltpu.VMEM((half, width, width), F32)] * 3,
+            *[pltpu.SemaphoreType.DMA((half,))] * 4,
+            *[pltpu.SemaphoreType.DMA((groups * (chips - 1),))] * 4,
+            *[pltpu.SemaphoreType.DMA((groups,))] * 2,
         ],
         compiler_params=pltpu.CompilerParams(
             collective_id=0, has_side_effects=True, vmem_limit_bytes=40 * 2**20

time: 105 us -> 81.3 us (0.77)
  Pallas kernels: 99.6 us -> 75.2 us
    pallas_call x1, Pallas kernels: 99.6 us -> 75.2 us  [shards(): pl.pallas_call(functools.partial(kernel, outer, inner), out_shape=jax.Sha...]
where the time goes in v1:
time: 81.3 us; the launch traced here: 80.2 us
  Pallas kernels  75.2 us (92%)
  local copies, waits for them, and re-layouts  4.31 us (5%)
    pallas_call x1, Pallas kernels, shards(): pl.pallas_call(functools.partial(kernel, outer, inner), out_shape=jax.Sha...  75.2 us
    unnamed x5, local copies, waits for them, and re-layouts  1.84 us
    transpose x1, local copies, waits for them, and re-layouts, shards(): return jnp.transpose(mixed, (1, 0, 2))  1.65 us

profile of v1, /device:TPU:31, one launch (start us, length us, event | category | flops | bytes accessed | tf_op | source)
XLA Modules:
  0.0 80.2 jit_solution(11036030726524643311)
XLA Ops:
  0.0 0.7 reshape.9
  0.7 0.0 copy-start
  0.7 0.0 copy-start.1
  0.7 1.8 %copy.12 = bf16[128,32,128]{2,0,1:T(8,128)(2,1)S(1)} copy(bf16[128,32,128]{2,1,0:T(8,128)(2,1)} %param.4) | data formatting | bytes 2097152 | tf_op args[0]
  2.5 0.0 copy-done
  2.5 0.1 copy-done.1
  2.6 0.8 %copy_bitcast_fusion = (bf16[32,128,128]{2,1,0:T(8,128)(2,1)S(1)}, bf16[32,128,128]{2,1,0:T(8,128)(2,1)S(1)}) fusion(bf16[128,32,128]{2,1,0:T(8,128)(2,1)S(1)} %copy-done, bf16[128,32,128]{2,1,0:T(8,128)(2,1)S(1)} %copy-done.1), kind=kLoop, calls=%fused_computation | loop fusion | bytes 4194304 | tf_op jit(solution)/shard_map/transpose | solution.py:321
  3.4 75.2 %shard_map.46 = bf16[32,128,128]{2,1,0:T(8,128)(2,1)S(1)} custom-call(bf16[32,128,128]{2,1,0:T(8,128)(2,1)S(1)} %bitcast.11, bf16[32,128,128]{2,1,0:T(8,128)(2,1)S(1)} %get-tuple-element.6.k_ref, bf16[32,128,128]{2,1,0:T(8,128)(2,1)S(1)} %get-tuple-element.5.v_ref, f32[32,1,128]{2,1,0:T(1,128)S(1)} %bitcast.13), custom_call_target="tpu_custom_call" | custom-call | flops 8053063680 | bytes 4194304 | tf_op jit(solution)/shard_map/pallas_call | solution.py:326
  78.6 1.6 %copy.8 = bf16[128,32,128]{2,1,0:T(8,128)(2,1)} copy(bf16[128,32,128]{2,0,1:T(8,128)(2,1)S(1)} %bitcast.12) | data formatting | bytes 2097152 | tf_op jit(solution)/shard_map/transpose | solution.py:355
Async XLA Ops:
  0.7 1.8 %copy-start = (bf16[128,32,128]{2,1,0:T(8,128)(2,1)S(1)}, bf16[128,32,128]{2,1,0:T(8,128)(2,1)}, u32[]{:S(2)}) copy-start(bf16[128,32,128]{2,1,0:T(8,128)(2,1)} %param.6) | copy-start | bytes 3145732
  0.7 1.9 %copy-start.1 = (bf16[128,32,128]{2,1,0:T(8,128)(2,1)S(1)}, bf16[128,32,128]{2,1,0:T(8,128)(2,1)}, u32[]{:S(2)}) copy-start(bf16[128,32,128]{2,1,0:T(8,128)(2,1)} %param.5) | copy-start | bytes 3145732

commit v2 on v1

--- a/solution.py
+++ b/solution.py
@@ -8,6 +8,7 @@
 from jax.sharding import PartitionSpec as P
 
 SPAN = 128
+BASE = 16
 F32 = jnp.float32
 BF16 = jnp.bfloat16
 
@@ -31,7 +32,45 @@
     return dot(jnp.concatenate([ah, al], 1), jnp.concatenate([b, b], 0))
 
 
-def block_map(keys, value, brow, rows, cols):
+def odd_rows(x, size):
+    return jnp.concatenate([x[at : at + size] for at in range(size, SPAN, 2 * size)], 0)
+
+
+def below(x, size):
+    shape = (SPAN // 2, SPAN)
+    block = lax.broadcasted_iota(jnp.int32, shape, 0) // size
+    return jnp.where(lax.broadcasted_iota(jnp.int32, shape, 1) // size == 2 * block, odd_rows(x, size), jnp.zeros((), x.dtype))
+
+
+def spaced(x, size):
+    zeros = jnp.zeros((size, x.shape[1]), x.dtype)
+    return jnp.concatenate([y for at in range(0, SPAN // 2, size) for y in (zeros, x[at : at + size])], 0)
+
+
+def minus_odd_rows(x, change, size):
+    out = []
+    for at in range(0, SPAN // 2, size):
+        out += [x[2 * at : 2 * at + size], x[2 * at + size : 2 * at + 2 * size] - change[at : at + size]]
+    return jnp.concatenate(out, 0)
+
+
+def diagonal_inverses(lower, pick):
+    count = len(lower)
+    row, lane = (lax.broadcasted_iota(jnp.int32, (BASE, SPAN), axis) for axis in (0, 1))
+    here = [lane // BASE == k for k in range(SPAN // BASE)]
+    beside = [sum(jnp.where(here[k], x[k * BASE : (k + 1) * BASE], 0.0) for k in range(SPAN // BASE)) for x in lower]
+    split = [halves(x) for x in beside]
+    spread = dot(jnp.concatenate([x for x, _ in split] + [x for _, x in split], 0), pick[...])
+    spread = spread[: count * BASE] + spread[count * BASE :]
+    found = [jnp.where(lane % BASE == row, 1.0, 0.0)] * count
+    for c in range(BASE - 1):
+        for i in range(count):
+            factor = spread[i * BASE : (i + 1) * BASE, c * SPAN : (c + 1) * SPAN]
+            found[i] = found[i] - factor * found[i][c : c + 1]
+    return [jnp.concatenate([jnp.where(x, y, 0.0) for x in here], 0) for y in found]
+
+
+def block_map(keys, value, brow, rows, cols, pick):
     eye = rows == cols
     width = keys[0].shape[1]
     count = range(len(keys))
@@ -41,37 +80,25 @@
     kcol = [lax.rsqrt(jnp.sum(x * x, axis=1, keepdims=True) + 1e-6) for x in kf]
     bcol = [jnp.sum(jnp.where(eye, x, 0.0), axis=1, keepdims=True) for x in brow]
     lower = [jnp.where(rows > cols, gram[i] * (bcol[i] * kcol[i]) * krow[i], 0.0) for i in count]
+    inverse = diagonal_inverses(lower, pick)
     split = [halves(x) for x in lower]
-
-    def merge_mask(level):
-        return ((rows >> (level + 1)) == (cols >> (level + 1))) & (((rows >> level) & 1) == 1) & (((cols >> level) & 1) == 0)
-
-    first = merge_mask(0)
-    inverse = [jnp.where(eye, 1.0, 0.0) - jnp.where(first, x, 0.0) for x in lower]
-    zero = jnp.zeros((), BF16)
-    for level in range(1, (SPAN - 1).bit_length()):
-        mask = merge_mask(level)
-        part = [(jnp.where(mask, h, zero), jnp.where(mask, l, zero)) for h, l in split]
+    size = BASE
+    while size < SPAN:
         inv = [halves(x) for x in inverse]
-        inner = [dot_halves(part[i], inv[i]) for i in count]
-        inner = [halves(x) for x in inner]
-        change = [dot_halves(inv[i], inner[i]) for i in count]
-        inverse = [inverse[i] - change[i] for i in count]
+        part = [tuple(below(x, size) for x in y) for y in split]
+        inner = [halves(dot_halves(part[i], inv[i])) for i in count]
+        inner = [tuple(spaced(x, size) for x in y) for y in inner]
+        change = [dot_halves(tuple(odd_rows(x, size) for x in inv[i]), inner[i]) for i in count]
+        inverse = [minus_odd_rows(inverse[i], change[i], size) for i in count]
+        size *= 2
     for_keys = [halves(inverse[i] * (brow[i] * krow[i])) for i in count]
     for_value = [halves(inverse[i] * brow[i]) for i in count]
     weights = [dot_exact(for_keys[i], keys[i]) for i in count]
     updates = [dot_exact(for_value[i], value[i]) for i in count]
     solved = [jnp.concatenate([weights[i], updates[i]], 1) for i in count]
     scaled = [halves(solved[i] * kcol[i]) for i in count]
-    written = [
-        lax.dot_general(
-            jnp.concatenate([keys[i], keys[i]], 0),
-            jnp.concatenate(scaled[i], 0),
-            (((0,), (0,)), ((), ())),
-            preferred_element_type=F32,
-        )
-        for i in count
-    ]
+    turned = [jnp.transpose(x) for x in keys]
+    written = [dot(jnp.concatenate([turned[i]] * 2, 1), jnp.concatenate(scaled[i], 0)) for i in count]
     trans = [jnp.where(eye, 1.0, 0.0) - x[:, :width] for x in written]
     return trans, [x[:, width:] for x in written], solved, krow
 
@@ -92,7 +119,7 @@
 
 def kernel(
     outer, inner, q_ref, k_ref, v_ref, b_ref, o_ref,
-    pair, outgoing, solved, norms, first, chip_map, cross, whole, jump, inside, came, goes, start, chip_start, middle, side,
+    pair, outgoing, solved, norms, first, chip_map, cross, whole, jump, inside, came, goes, start, chip_start, middle, side, pick,
     ab_send, ab_recv, side_send, side_recv, cross_send, cross_recv, down_send, down_recv, chain_send, chain_recv,
 ):
     heads = q_ref.shape[0]
@@ -159,6 +186,10 @@
     def masks():
         return [lax.broadcasted_iota(jnp.int32, (SPAN, SPAN), axis) for axis in (0, 1)]
 
+    row, lane = masks()
+    for c in range(BASE - 1):
+        pick[:, c * SPAN : (c + 1) * SPAN] = jnp.where(row == lane // BASE * BASE + c, 1.0, 0.0).astype(BF16)
+
     def group(g):
         ms = [c * groups + g for c in range(chips)]
         return ms, [core * owned + m for m in ms], [(1 - core) * owned + m for m in ms]
@@ -166,7 +197,7 @@
     def prepare(g):
         ms, mine, theirs = group(g)
         hs = mine + theirs
-        a, b, wu, krow = block_map(*([ref[h] for h in hs] for ref in (k_ref, v_ref, b_ref)), *masks())
+        a, b, wu, krow = block_map(*([ref[h] for h in hs] for ref in (k_ref, v_ref, b_ref)), *masks(), pick)
         for j, h in enumerate(hs):
             solved[h] = wu[j]
             norms[h] = krow[j]
@@ -343,6 +374,7 @@
             pltpu.VMEM((groups, width, width), F32),
             pltpu.VMEM((groups, chips, width, width), F32),
             *[pltpu.VMEM((half, width, width), F32)] * 3,
+            pltpu.VMEM((SPAN, (BASE - 1) * SPAN), BF16),
             *[pltpu.SemaphoreType.DMA((half,))] * 4,
             *[pltpu.SemaphoreType.DMA((groups * (chips - 1),))] * 4,
             *[pltpu.SemaphoreType.DMA((groups,))] * 2,

time: 81.3 us -> 77.8 us (0.957)
  Pallas kernels: 75.2 us -> 72.1 us
    pallas_call x1, Pallas kernels: 75.2 us -> 72.1 us  [shards(): pl.pallas_call(functools.partial(kernel, outer, inner), out_shape=jax.Sha...]
where the time goes in v2:
time: 77.8 us; the launch traced here: 77.1 us
  Pallas kernels  72.1 us (93%)
  local copies, waits for them, and re-layouts  4.31 us (6%)
    pallas_call x1, Pallas kernels, shards(): pl.pallas_call(functools.partial(kernel, outer, inner), out_shape=jax.Sha...  72.1 us
    unnamed x5, local copies, waits for them, and re-layouts  1.84 us
    transpose x1, local copies, waits for them, and re-layouts, shards(): return jnp.transpose(mixed, (1, 0, 2))  1.65 us

profile of v2, /device:TPU:31, one launch (start us, length us, event | category | flops | bytes accessed | tf_op | source)
XLA Modules:
  0.0 77.1 jit_solution(4805211602568064410)
XLA Ops:
  0.0 0.7 reshape.9
  0.7 0.0 copy-start
  0.7 0.0 copy-start.1
  0.7 1.8 %copy.12 = bf16[128,32,128]{2,0,1:T(8,128)(2,1)S(1)} copy(bf16[128,32,128]{2,1,0:T(8,128)(2,1)} %param.4) | data formatting | bytes 2097152 | tf_op args[0]
  2.5 0.0 copy-done
  2.5 0.1 copy-done.1
  2.6 0.8 %copy_bitcast_fusion = (bf16[32,128,128]{2,1,0:T(8,128)(2,1)S(1)}, bf16[32,128,128]{2,1,0:T(8,128)(2,1)S(1)}) fusion(bf16[128,32,128]{2,1,0:T(8,128)(2,1)S(1)} %copy-done, bf16[128,32,128]{2,1,0:T(8,128)(2,1)S(1)} %copy-done.1), kind=kLoop, calls=%fused_computation | loop fusion | bytes 4194304 | tf_op jit(solution)/shard_map/transpose | solution.py:352
  3.4 72.1 %shard_map.46 = bf16[32,128,128]{2,1,0:T(8,128)(2,1)S(1)} custom-call(bf16[32,128,128]{2,1,0:T(8,128)(2,1)S(1)} %bitcast.11, bf16[32,128,128]{2,1,0:T(8,128)(2,1)S(1)} %get-tuple-element.6.k_ref, bf16[32,128,128]{2,1,0:T(8,128)(2,1)S(1)} %get-tuple-element.5.v_ref, f32[32,1,128]{2,1,0:T(1,128)S(1)} %bitcast.13), custom_call_target="tpu_custom_call" | custom-call | flops 8053063680 | bytes 4194304 | tf_op jit(solution)/shard_map/pallas_call | solution.py:357
  75.5 1.6 %copy.8 = bf16[128,32,128]{2,1,0:T(8,128)(2,1)} copy(bf16[128,32,128]{2,0,1:T(8,128)(2,1)S(1)} %bitcast.12) | data formatting | bytes 2097152 | tf_op jit(solution)/shard_map/transpose | solution.py:387
Async XLA Ops:
  0.7 1.8 %copy-start = (bf16[128,32,128]{2,1,0:T(8,128)(2,1)S(1)}, bf16[128,32,128]{2,1,0:T(8,128)(2,1)}, u32[]{:S(2)}) copy-start(bf16[128,32,128]{2,1,0:T(8,128)(2,1)} %param.6) | copy-start | bytes 3145732
  0.7 1.9 %copy-start.1 = (bf16[128,32,128]{2,1,0:T(8,128)(2,1)S(1)}, bf16[128,32,128]{2,1,0:T(8,128)(2,1)}, u32[]{:S(2)}) copy-start(bf16[128,32,128]{2,1,0:T(8,128)(2,1)} %param.5) | copy-start | bytes 3145732

commit v3 on v2

--- a/solution.py
+++ b/solution.py
@@ -258,6 +258,8 @@
         def _():
             hop(g).start()
 
+    def descend(g):
+        state = came[g]
         for c in range(chips):
             start[g, c] = state
             if c < chips - 1:
@@ -305,9 +307,10 @@
             aside(middle, m).wait_recv()
         put(theirs, [side[m] for m in ms])
 
-    ahead = jnp.minimum(groups, 2 + 3 * stage // 4)
-    late = jnp.where(stage < outer // 4, groups + ahead, 0)
-    last = jnp.maximum(late, ahead + 2)
+    ahead = jnp.minimum(groups, 2 + stage)
+    busy = stage < 5 * outer // 8
+    late = jnp.where(stage < outer // 4, groups + ahead, jnp.where(busy, groups, 0))
+    below_at = jnp.maximum(late, ahead)
 
     def step(i, carry):
         def at(delay, do):
@@ -316,15 +319,16 @@
                 do(i - delay)
 
         at(0, prepare)
-        at(late, read_terms)
         at(1, compose)
         at(2, compose_chips)
         at(ahead, pass_on)
-        at(ahead + 1, spread)
-        at(last, finish)
+        at(late, read_terms)
+        at(below_at, descend)
+        at(below_at + 1, spread)
+        at(below_at + 2, finish)
         return carry
 
-    lax.fori_loop(0, groups + last, step, 0)
+    lax.fori_loop(0, groups + below_at + 2, step, 0)
 
     def drain(m, carry):
         give(m).wait_send()

time: 77.8 us -> 72.7 us (0.934)
  Pallas kernels: 72.1 us -> 66.5 us
    pallas_call x1, Pallas kernels: 72.1 us -> 66.5 us  [shards(): pl.pallas_call(functools.partial(kernel, outer, inner), out_shape=jax.Sha...]
where the time goes in v3:
time: 72.7 us; the launch traced here: 71.5 us
  Pallas kernels  66.5 us (91%)
  local copies, waits for them, and re-layouts  4.31 us (6%)
    pallas_call x1, Pallas kernels, shards(): pl.pallas_call(functools.partial(kernel, outer, inner), out_shape=jax.Sha...  66.5 us
    unnamed x5, local copies, waits for them, and re-layouts  1.84 us
    transpose x1, local copies, waits for them, and re-layouts, shards(): return jnp.transpose(mixed, (1, 0, 2))  1.65 us

profile of v3, /device:TPU:31, one launch (start us, length us, event | category | flops | bytes accessed | tf_op | source)
XLA Modules:
  0.0 71.5 jit_solution(17786362377662424457)
XLA Ops:
  0.0 0.7 reshape.9
  0.7 0.0 copy-start
  0.7 0.0 copy-start.1
  0.7 1.8 %copy.12 = bf16[128,32,128]{2,0,1:T(8,128)(2,1)S(1)} copy(bf16[128,32,128]{2,1,0:T(8,128)(2,1)} %param.4) | data formatting | bytes 2097152 | tf_op args[0]
  2.5 0.0 copy-done
  2.5 0.1 copy-done.1
  2.6 0.8 %copy_bitcast_fusion = (bf16[32,128,128]{2,1,0:T(8,128)(2,1)S(1)}, bf16[32,128,128]{2,1,0:T(8,128)(2,1)S(1)}) fusion(bf16[128,32,128]{2,1,0:T(8,128)(2,1)S(1)} %copy-done, bf16[128,32,128]{2,1,0:T(8,128)(2,1)S(1)} %copy-done.1), kind=kLoop, calls=%fused_computation | loop fusion | bytes 4194304 | tf_op jit(solution)/shard_map/transpose | solution.py:356
  3.4 66.5 %shard_map.46 = bf16[32,128,128]{2,1,0:T(8,128)(2,1)S(1)} custom-call(bf16[32,128,128]{2,1,0:T(8,128)(2,1)S(1)} %bitcast.11, bf16[32,128,128]{2,1,0:T(8,128)(2,1)S(1)} %get-tuple-element.6.k_ref, bf16[32,128,128]{2,1,0:T(8,128)(2,1)S(1)} %get-tuple-element.5.v_ref, f32[32,1,128]{2,1,0:T(1,128)S(1)} %bitcast.13), custom_call_target="tpu_custom_call" | custom-call | flops 8053063680 | bytes 4194304 | tf_op jit(solution)/shard_map/pallas_call | solution.py:361
  69.9 1.6 %copy.8 = bf16[128,32,128]{2,1,0:T(8,128)(2,1)} copy(bf16[128,32,128]{2,0,1:T(8,128)(2,1)S(1)} %bitcast.12) | data formatting | bytes 2097152 | tf_op jit(solution)/shard_map/transpose | solution.py:391
Async XLA Ops:
  0.7 1.8 %copy-start = (bf16[128,32,128]{2,1,0:T(8,128)(2,1)S(1)}, bf16[128,32,128]{2,1,0:T(8,128)(2,1)}, u32[]{:S(2)}) copy-start(bf16[128,32,128]{2,1,0:T(8,128)(2,1)} %param.6) | copy-start | bytes 3145732
  0.7 1.9 %copy-start.1 = (bf16[128,32,128]{2,1,0:T(8,128)(2,1)S(1)}, bf16[128,32,128]{2,1,0:T(8,128)(2,1)}, u32[]{:S(2)}) copy-start(bf16[128,32,128]{2,1,0:T(8,128)(2,1)} %param.5) | copy-start | bytes 3145732

commit v4 on v3

--- a/solution.py
+++ b/solution.py
@@ -74,18 +74,24 @@
     eye = rows == cols
     width = keys[0].shape[1]
     count = range(len(keys))
-    gram = [lax.dot_general(x, x, (((1,), (1,)), ((), ())), preferred_element_type=F32) for x in keys]
+    ones = jnp.where(eye, 1.0, 0.0).astype(BF16)
+    both = [
+        lax.dot_general(
+            jnp.concatenate([x, ones], 0), x, (((1,), (1,)), ((), ())), preferred_element_type=F32
+        )
+        for x in keys
+    ]
+    gram, turned = [x[:SPAN] for x in both], [x[SPAN:].astype(BF16) for x in both]
     kf = [x.astype(F32) for x in keys]
     krow = [lax.rsqrt(jnp.sum(jnp.where(eye, x, 0.0), axis=0, keepdims=True) + 1e-6) for x in gram]
     kcol = [lax.rsqrt(jnp.sum(x * x, axis=1, keepdims=True) + 1e-6) for x in kf]
     bcol = [jnp.sum(jnp.where(eye, x, 0.0), axis=1, keepdims=True) for x in brow]
     lower = [jnp.where(rows > cols, gram[i] * (bcol[i] * kcol[i]) * krow[i], 0.0) for i in count]
     inverse = diagonal_inverses(lower, pick)
-    split = [halves(x) for x in lower]
     size = BASE
     while size < SPAN:
         inv = [halves(x) for x in inverse]
-        part = [tuple(below(x, size) for x in y) for y in split]
+        part = [halves(below(x, size)) for x in lower]
         inner = [halves(dot_halves(part[i], inv[i])) for i in count]
         inner = [tuple(spaced(x, size) for x in y) for y in inner]
         change = [dot_halves(tuple(odd_rows(x, size) for x in inv[i]), inner[i]) for i in count]
@@ -97,7 +103,6 @@
     updates = [dot_exact(for_value[i], value[i]) for i in count]
     solved = [jnp.concatenate([weights[i], updates[i]], 1) for i in count]
     scaled = [halves(solved[i] * kcol[i]) for i in count]
-    turned = [jnp.transpose(x) for x in keys]
     written = [dot(jnp.concatenate([turned[i]] * 2, 1), jnp.concatenate(scaled[i], 0)) for i in count]
     trans = [jnp.where(eye, 1.0, 0.0) - x[:, :width] for x in written]
     return trans, [x[:, width:] for x in written], solved, krow
@@ -251,11 +256,9 @@
         def _():
             hop(g).wait_recv()
 
-        state = came[g]
-        goes[g] = apply(whole[g], state, jump[g])
-
         @pl.when(stage < outer - 1)
         def _():
+            goes[g] = apply(whole[g], came[g], jump[g])
             hop(g).start()
 
     def descend(g):

time: 72.7 us -> 72.6 us (level)
  no operation moved by 1% of the time
where the time goes in v4:
time: 72.6 us; the launch traced here: 71.4 us
  Pallas kernels  66.3 us (91%)
  local copies, waits for them, and re-layouts  4.31 us (6%)
    pallas_call x1, Pallas kernels, shards(): pl.pallas_call(functools.partial(kernel, outer, inner), out_shape=jax.Sha...  66.3 us
    unnamed x5, local copies, waits for them, and re-layouts  1.84 us
    transpose x1, local copies, waits for them, and re-layouts, shards(): return jnp.transpose(mixed, (1, 0, 2))  1.65 us

profile of v4, /device:TPU:31, one launch (start us, length us, event | category | flops | bytes accessed | tf_op | source)
XLA Modules:
  0.0 71.4 jit_solution(13840646893146193339)
XLA Ops:
  0.0 0.7 reshape.9
  0.7 0.0 copy-start
  0.7 0.0 copy-start.1
  0.7 1.8 %copy.12 = bf16[128,32,128]{2,0,1:T(8,128)(2,1)S(1)} copy(bf16[128,32,128]{2,1,0:T(8,128)(2,1)} %param.4) | data formatting | bytes 2097152 | tf_op args[0]
  2.5 0.0 copy-done
  2.5 0.1 copy-done.1
  2.6 0.8 %copy_bitcast_fusion = (bf16[32,128,128]{2,1,0:T(8,128)(2,1)S(1)}, bf16[32,128,128]{2,1,0:T(8,128)(2,1)S(1)}) fusion(bf16[128,32,128]{2,1,0:T(8,128)(2,1)S(1)} %copy-done, bf16[128,32,128]{2,1,0:T(8,128)(2,1)S(1)} %copy-done.1), kind=kLoop, calls=%fused_computation | loop fusion | bytes 4194304 | tf_op jit(solution)/shard_map/transpose | solution.py:359
  3.4 66.3 %shard_map.46 = bf16[32,128,128]{2,1,0:T(8,128)(2,1)S(1)} custom-call(bf16[32,128,128]{2,1,0:T(8,128)(2,1)S(1)} %bitcast.11, bf16[32,128,128]{2,1,0:T(8,128)(2,1)S(1)} %get-tuple-element.6.k_ref, bf16[32,128,128]{2,1,0:T(8,128)(2,1)S(1)} %get-tuple-element.5.v_ref, f32[32,1,128]{2,1,0:T(1,128)S(1)} %bitcast.13), custom_call_target="tpu_custom_call" | custom-call | flops 8053063680 | bytes 4194304 | tf_op jit(solution)/shard_map/pallas_call | solution.py:364
  69.7 1.6 %copy.8 = bf16[128,32,128]{2,1,0:T(8,128)(2,1)} copy(bf16[128,32,128]{2,0,1:T(8,128)(2,1)S(1)} %bitcast.12) | data formatting | bytes 2097152 | tf_op jit(solution)/shard_map/transpose | solution.py:394
Async XLA Ops:
  0.7 1.8 %copy-start = (bf16[128,32,128]{2,1,0:T(8,128)(2,1)S(1)}, bf16[128,32,128]{2,1,0:T(8,128)(2,1)}, u32[]{:S(2)}) copy-start(bf16[128,32,128]{2,1,0:T(8,128)(2,1)} %param.6) | copy-start | bytes 3145732
  0.7 1.9 %copy-start.1 = (bf16[128,32,128]{2,1,0:T(8,128)(2,1)S(1)}, bf16[128,32,128]{2,1,0:T(8,128)(2,1)}, u32[]{:S(2)}) copy-start(bf16[128,32,128]{2,1,0:T(8,128)(2,1)} %param.5) | copy-start | bytes 3145732

commit v5 on v4

--- a/solution.py
+++ b/solution.py
@@ -310,7 +310,7 @@
             aside(middle, m).wait_recv()
         put(theirs, [side[m] for m in ms])
 
-    ahead = jnp.minimum(groups, 2 + stage)
+    ahead = jnp.maximum(4, jnp.minimum(groups, 4 + stage))
     busy = stage < 5 * outer // 8
     late = jnp.where(stage < outer // 4, groups + ahead, jnp.where(busy, groups, 0))
     below_at = jnp.maximum(late, ahead)
@@ -322,8 +322,8 @@
                 do(i - delay)
 
         at(0, prepare)
-        at(1, compose)
-        at(2, compose_chips)
+        at(2, compose)
+        at(4, compose_chips)
         at(ahead, pass_on)
         at(late, read_terms)
         at(below_at, descend)

time: 72.6 us -> 71.6 us (0.986); the launches traced: 71.4 us -> 71.3 us
  no operation moved by 1% of the time
where the time goes in v5:
time: 71.6 us; the launch traced here: 71.3 us
  Pallas kernels  66.2 us (92%)
  local copies, waits for them, and re-layouts  4.31 us (6%)
    pallas_call x1, Pallas kernels, shards(): pl.pallas_call(functools.partial(kernel, outer, inner), out_shape=jax.Sha...  66.2 us
    unnamed x5, local copies, waits for them, and re-layouts  1.84 us
    transpose x1, local copies, waits for them, and re-layouts, shards(): return jnp.transpose(mixed, (1, 0, 2))  1.65 us

profile of v5, /device:TPU:31, one launch (start us, length us, event | category | flops | bytes accessed | tf_op | source)
XLA Modules:
  0.0 71.3 jit_solution(12599408305638930050)
XLA Ops:
  0.0 0.7 reshape.9
  0.7 0.0 copy-start
  0.7 0.0 copy-start.1
  0.7 1.8 %copy.12 = bf16[128,32,128]{2,0,1:T(8,128)(2,1)S(1)} copy(bf16[128,32,128]{2,1,0:T(8,128)(2,1)} %param.4) | data formatting | bytes 2097152 | tf_op args[0]
  2.5 0.0 copy-done
  2.5 0.1 copy-done.1
  2.6 0.8 %copy_bitcast_fusion = (bf16[32,128,128]{2,1,0:T(8,128)(2,1)S(1)}, bf16[32,128,128]{2,1,0:T(8,128)(2,1)S(1)}) fusion(bf16[128,32,128]{2,1,0:T(8,128)(2,1)S(1)} %copy-done, bf16[128,32,128]{2,1,0:T(8,128)(2,1)S(1)} %copy-done.1), kind=kLoop, calls=%fused_computation | loop fusion | bytes 4194304 | tf_op jit(solution)/shard_map/transpose | solution.py:359
  3.4 66.2 %shard_map.46 = bf16[32,128,128]{2,1,0:T(8,128)(2,1)S(1)} custom-call(bf16[32,128,128]{2,1,0:T(8,128)(2,1)S(1)} %bitcast.11, bf16[32,128,128]{2,1,0:T(8,128)(2,1)S(1)} %get-tuple-element.6.k_ref, bf16[32,128,128]{2,1,0:T(8,128)(2,1)S(1)} %get-tuple-element.5.v_ref, f32[32,1,128]{2,1,0:T(1,128)S(1)} %bitcast.13), custom_call_target="tpu_custom_call" | custom-call | flops 8053063680 | bytes 4194304 | tf_op jit(solution)/shard_map/pallas_call | solution.py:364
  69.6 1.6 %copy.8 = bf16[128,32,128]{2,1,0:T(8,128)(2,1)} copy(bf16[128,32,128]{2,0,1:T(8,128)(2,1)S(1)} %bitcast.12) | data formatting | bytes 2097152 | tf_op jit(solution)/shard_map/transpose | solution.py:394
Async XLA Ops:
  0.7 1.8 %copy-start = (bf16[128,32,128]{2,1,0:T(8,128)(2,1)S(1)}, bf16[128,32,128]{2,1,0:T(8,128)(2,1)}, u32[]{:S(2)}) copy-start(bf16[128,32,128]{2,1,0:T(8,128)(2,1)} %param.6) | copy-start | bytes 3145732
  0.7 1.9 %copy-start.1 = (bf16[128,32,128]{2,1,0:T(8,128)(2,1)S(1)}, bf16[128,32,128]{2,1,0:T(8,128)(2,1)}, u32[]{:S(2)}) copy-start(bf16[128,32,128]{2,1,0:T(8,128)(2,1)} %param.5) | copy-start | bytes 3145732
